TPU v7x, 512 devices: a whole 4x8x8 slice. The times are simulated.
512 devices in a mesh: dom: 128 (over z, y, core), hub: 4 (over x).
Axes of the slice: x: 4, y: 8, z: 8, core: 2. Of those that a mesh axis runs over, the one named last changes fastest.
Arguments:
- user_cot: float32 [16384, 256], P('dom'), may hold values from -6 to 6
- hub_adj: float32 [16384, 2048], P('dom', 'hub'), may hold values from -0.09375 to 0.09375
- tiles: float32 [65536, 8, 128], P(('dom', 'hub')), may hold values from -0.125 to 0.125
- tile_index: int32 [3, 65536], P(None, ('dom', 'hub')), may hold values from 0 to 127, as said below
- hub_mask: int32 [2, 2048, 256], P(None, 'hub'), may hold values 0 or 1
- tail_mask: int32 [2, 32768, 256], P(None, 'dom'), may hold values 0 or 1
Outputs:
- user_grad: float32 [16384, 256], P('dom')
- hub_grad: float32 [2048, 256], P('hub')
- tail_grad: float32 [32768, 256], P('dom')
Inputs may be any that keep to these rules, and one draw needn't show every extreme that they name: `tile_index`: row 0 is a tile's user block within its own partition (below 1), row 1 the partition that owns its items (below 128 partitions, i.e. 16384 / 128), row 2 the item block within that partition (below 32). Rows 1 and 2 are the same, position by position, on all 4 hub shards of one partition. No device holds more than 2 tiles whose items one partition owns. One particular partition receives exactly 2 tiles from every device; any other partition receives 0, 1 or 2 tiles from a device.
All inputs are finite; a program needn't handle non-finite values. No bound on the sum of `hub_mask` or of `tail_mask` on one device may be relied on, other than what follows from the above.
Results may differ from a plain program's by a relative error of at most 0.0001.
Values sent between devices are 32-bit elements; how exact they have to be, the bound alone decides.
A program may use at most 64 MiB of HBM per device.

v0:
```python
import jax
import jax.numpy as jnp
from jax import lax
from jax.sharding import PartitionSpec as P

PRECISE = lax.Precision.HIGHEST


def local(user_cot, hub_adj, tiles, tile_index, hub_mask, tail_mask):
    dom_count = lax.axis_size("dom")
    tile_count, item_rows, user_rows = tiles.shape
    user_count, feature_width = user_cot.shape
    user_blocks = user_count // user_rows
    tail_rows = tail_mask.shape[1]
    tail_blocks = tail_rows // item_rows
    capacity = max(2, 2 * tile_count // dom_count)
    slot_count = dom_count * capacity
    user_block = tile_index[0]
    owners = tile_index[1]
    item_block = tile_index[2]
    chosen = (user_block[:, None] == jnp.arange(user_blocks, dtype=jnp.int32)[None, :]).astype(
        jnp.float32
    )
    placed = (chosen[:, None, :, None] * tiles[:, :, None, :]).reshape(
        tile_count * item_rows, user_count
    )
    positions = jnp.arange(tile_count, dtype=jnp.int32)
    before = (owners[:, None] == owners[None, :]) & (positions[None, :] < positions[:, None])
    ranks = jnp.sum(before.astype(jnp.int32), axis=1)
    slot_of = owners * capacity + ranks
    slot_block = jnp.zeros((slot_count,), jnp.int32).at[slot_of].set(item_block)
    block_ids = jnp.arange(tail_blocks, dtype=jnp.int32)
    gradient = user_cot
    hub_item = None
    tail_item = None
    for trip_index in range(hub_mask.shape[0]):
        hub_part = lax.dot_general(
            hub_adj,
            gradient,
            (((0,), (0,)), ((), ())),
            precision=PRECISE,
            preferred_element_type=jnp.float32,
        )
        hub_item = lax.psum(hub_part, "dom") * hub_mask[trip_index].astype(jnp.float32)
        tile_part = jnp.dot(placed, gradient, precision=PRECISE, preferred_element_type=jnp.float32)
        tile_part = tile_part.reshape(tile_count, item_rows * feature_width)
        outgoing = (
            jnp.zeros((slot_count, item_rows * feature_width), jnp.float32)
            .at[slot_of]
            .set(tile_part)
        )
        incoming, got_block = (
            lax.all_to_all(outgoing, "dom", split_axis=0, concat_axis=0, tiled=True),
            lax.all_to_all(slot_block, "dom", split_axis=0, concat_axis=0, tiled=True),
        )
        member = (got_block[None, :] == block_ids[:, None]).astype(jnp.float32)
        tail_part = jnp.dot(member, incoming, precision=PRECISE, preferred_element_type=jnp.float32)
        tail_part = tail_part.reshape(tail_rows, feature_width)
        tail_item = lax.psum(tail_part, "hub") * tail_mask[trip_index].astype(jnp.float32)
        answer = tail_item.reshape(tail_blocks, item_rows * feature_width)[got_block]
        returned = lax.all_to_all(answer, "dom", split_axis=0, concat_axis=0, tiled=True)
        tile_item = returned[slot_of].reshape(tile_count * item_rows, feature_width)
        user_part = jnp.dot(
            hub_adj, hub_item, precision=PRECISE, preferred_element_type=jnp.float32
        )
        user_part = user_part + lax.dot_general(
            placed,
            tile_item,
            (((0,), (0,)), ((), ())),
            precision=PRECISE,
            preferred_element_type=jnp.float32,
        )
        gradient = lax.psum(user_part, "hub")
    return (gradient, hub_item, tail_item)


def solution(mesh):
    return jax.shard_map(
        local,
        mesh=mesh,
        in_specs=(
            P("dom", None),
            P("dom", "hub"),
            P(("dom", "hub"), None, None),
            P(None, ("dom", "hub")),
            P(None, "hub", None),
            P(None, "dom", None),
        ),
        out_specs=(P("dom", None), P("hub", None), P("dom", None)),
        check_vma=False,
    )
```

profile of v0, /device:TPU:8, one launch (start us, length us, event | category | flops | bytes accessed | tf_op | source)
XLA Modules:
  0.0 877.5 jit_solution(14577120800041582356)
XLA Ops:
  9.6 1.0 scatter_custom_fusion
  11.4 17.4 %all-to-all-start = ((s32[128,2,1]{1,2,0:T(1,128)}), s32[128,2,1]{1,2,0:T(1,128)S(1)}, u32[]{:S(2)}, u32[]{:S(2)}) async-start(s32[128,2,1]{1,2,0:T(1,128)} %bitcast.9), calls=%async_computation | async-start | bytes 131072 | tf_op jit(solution)/shard_map/all_to_all | solution.py:54
  29.5 2.1 fusion.12
  31.7 1.7 scatter_custom_fusion.1
  33.4 2.3 all_to_all.43
  35.7 3.8 all-to-all-done
  39.5 10.0 %all-to-all-start.1 = ((f32[128,2,2048]{2,1,0:T(2,128)}), f32[128,2,2048]{2,1,0:T(2,128)S(1)}, u32[]{:S(2)}, u32[]{:S(2)}) async-start(f32[128,2,2048]{2,1,0:T(2,128)} %all_to_all.43), calls=%async_computation.1 | async-start | bytes 4194304 | tf_op jit(solution)/shard_map/all_to_all | solution.py:53
  50.1 0.8 reduce.5
  51.1 52.4 %all-to-all-done.1 = f32[128,2,2048]{2,1,0:T(2,128)S(1)} async-done(((f32[128,2,2048]{2,1,0:T(2,128)}), f32[128,2,2048]{2,1,0:T(2,128)S(1)}, u32[]{:S(2)}, u32[]{:S(2)}) %all-to-all-start.1) | async-done | bytes 2097184 | tf_op jit(solution)/shard_map/all_to_all | solution.py:53
  103.5 2.5 all_to_all.45
  106.0 2.5 fusion.26
  109.3 45.8 %all-reduce.9.cloned.1.call-done = f32[256,256]{1,0:T(8,128)} async-done(((f32[256,256]{1,0:T(8,128)}), f32[256,256]{1,0:T(8,128)}) %all-reduce.9.cloned.1.call-update) | async-done | bytes 262160 | tf_op jit(solution)/shard_map/psum | solution.py:59
  155.1 1.0 bitcast_multiply_fusion.4
  156.2 1.5 gather_fusion
  157.6 2.3 all_to_all.47
  159.9 14.9 %all-to-all-start.2 = ((f32[128,2,2048]{2,1,0:T(2,128)}), f32[128,2,2048]{2,1,0:T(2,128)}, u32[]{:S(2)}, u32[]{:S(2)}) async-start(f32[128,2,2048]{2,1,0:T(2,128)} %all_to_all.47), calls=%async_computation.2 | async-start | bytes 4194304 | tf_op jit(solution)/shard_map/all_to_all | solution.py:61
  174.9 1.4 fusion.33
  176.4 52.4 %all-to-all-done.2 = f32[128,2,2048]{2,1,0:T(2,128)} async-done(((f32[128,2,2048]{2,1,0:T(2,128)}), f32[128,2,2048]{2,1,0:T(2,128)}, u32[]{:S(2)}, u32[]{:S(2)}) %all-to-all-start.2) | async-done | bytes 2097184 | tf_op jit(solution)/shard_map/all_to_all | solution.py:61
  228.8 2.7 all_to_all.49
  231.5 1.9 gather_fusion.1
  233.4 1.5 reshape.128
  234.9 2.0 fusion.10
  236.9 155.1 %all-reduce.7.cloned.1.call-done = f32[512,256]{1,0:T(8,128)} async-done(((f32[512,256]{1,0:T(8,128)}), f32[512,256]{1,0:T(8,128)}) %all-reduce.7.cloned.1.call-update) | async-done | bytes 524304 | tf_op jit(solution)/shard_map/psum | solution.py:44
  392.0 2.7 fusion.1
  394.7 50.2 %all-reduce.11.cloned.1.call-done = f32[128,256]{0,1:T(8,128)} async-done(((f32[128,256]{0,1:T(8,128)}), f32[128,256]{0,1:T(8,128)}) %all-reduce.11.cloned.1.call-update) | async-done | bytes 131088 | tf_op jit(solution)/shard_map/psum | solution.py:73
  444.9 1.9 fusion.8
  446.8 1.1 reshape.186
  448.0 2.4 scatter_custom_fusion.2
  450.4 2.3 all_to_all.50
  452.7 68.3 %all_to_all.61 = f32[128,2,2048]{2,1,0:T(2,128)} all-to-all(f32[128,2,2048]{2,1,0:T(2,128)} %all_to_all.50), channel_id=1, replica_groups=mesh['dom'=128,'hub'=4] {'dom'}, dimensions={0} | all-to-all | bytes 4194304 | tf_op jit(solution)/shard_map/all_to_all | solution.py:53
  521.0 2.7 all_to_all.52
  523.7 0.9 fusion.25
  525.4 45.0 %all-reduce.15.cloned.1.call-done = f32[256,256]{1,0:T(8,128)} async-done(((f32[256,256]{1,0:T(8,128)}), f32[256,256]{1,0:T(8,128)}) %all-reduce.15.cloned.1.call-update) | async-done | bytes 262160 | tf_op jit(solution)/shard_map/psum | solution.py:59
  570.4 1.1 bitcast_multiply_fusion.3
  571.5 1.5 gather_fusion.2
  573.0 2.3 all_to_all.53
  575.3 14.7 %all-to-all-start.4 = ((f32[128,2,2048]{2,1,0:T(2,128)}), f32[128,2,2048]{2,1,0:T(2,128)}, u32[]{:S(2)}, u32[]{:S(2)}) async-start(f32[128,2,2048]{2,1,0:T(2,128)} %all_to_all.53), calls=%async_computation.4 | async-start | bytes 4194304 | tf_op jit(solution)/shard_map/all_to_all | solution.py:61
  590.1 1.4 convolution_bitcast_fusion
  591.7 215.6 %all-reduce.13.cloned.1.call-done = f32[512,256]{0,1:T(8,128)} async-done(((f32[512,256]{0,1:T(8,128)}), f32[512,256]{0,1:T(8,128)}) %all-reduce.13.cloned.1.call-update) | async-done | bytes 524304 | tf_op jit(solution)/shard_map/psum | solution.py:44
  807.3 1.9 bitcast_multiply_fusion
  809.3 2.7 all_to_all.55
  812.0 1.9 gather_fusion.3
  813.9 1.4 reshape.132
  815.3 2.0 fusion.6
  817.3 1.2 fusion
  818.6 1.0 copy.30
  819.5 49.2 %all-reduce.17.cloned.1.call-done = f32[128,256]{0,1:T(8,128)} async-done(((f32[128,256]{0,1:T(8,128)}), f32[128,256]{0,1:T(8,128)}) %all-reduce.17.cloned.1.call-update) | async-done | bytes 131088 | tf_op jit(solution)/shard_map/psum | solution.py:73
  868.7 1.7 copy.29
  (48 shorter events, 6.2 us)
Async XLA Ops:
  8.0 166.9 %copy-start = (f32[128,512]{1,0:T(8,128)S(1)}, f32[128,512]{1,0:T(8,128)}, u32[]{:S(2)}) copy-start(f32[128,512]{1,0:T(8,128)} %param.7) | copy-start | bytes 786436
  11.4 28.1 %all-to-all-start = ((s32[128,2,1]{1,2,0:T(1,128)}), s32[128,2,1]{1,2,0:T(1,128)S(1)}, u32[]{:S(2)}, u32[]{:S(2)}) async-start(s32[128,2,1]{1,2,0:T(1,128)} %bitcast.9), calls=%async_computation | async-start | bytes 131072 | tf_op jit(solution)/shard_map/all_to_all | solution.py:54
  39.5 64.0 %all-to-all-start.1 = ((f32[128,2,2048]{2,1,0:T(2,128)}), f32[128,2,2048]{2,1,0:T(2,128)S(1)}, u32[]{:S(2)}, u32[]{:S(2)}) async-start(f32[128,2,2048]{2,1,0:T(2,128)} %all_to_all.43), calls=%async_computation.1 | async-start | bytes 4194304 | tf_op jit(solution)/shard_map/all_to_all | solution.py:53
  49.5 105.6 %all-reduce.9.cloned.1.call-start = ((), (), s32[]{:S(2)}) async-start(), calls=%async_computation.6 | async-start | bytes 524288 | tf_op jit(solution)/shard_map/psum | solution.py:59
  106.0 49.1 %copy-start.5 = (s32[2,256,256]{2,1,0:T(8,128)S(1)}, s32[2,256,256]{2,1,0:T(8,128)}, u32[]{:S(2)}) copy-start(s32[2,256,256]{2,1,0:T(8,128)} %param.11) | copy-start | bytes 1572868
  159.9 15.0 %copy-start.6 = (f32[128,256]{1,0:T(8,128)S(1)}, f32[128,256]{1,0:T(8,128)}, u32[]{:S(2)}) copy-start(f32[128,256]{1,0:T(8,128)} %param.6) | copy-start | bytes 393220
  159.9 68.9 %all-to-all-start.2 = ((f32[128,2,2048]{2,1,0:T(2,128)}), f32[128,2,2048]{2,1,0:T(2,128)}, u32[]{:S(2)}, u32[]{:S(2)}) async-start(f32[128,2,2048]{2,1,0:T(2,128)} %all_to_all.47), calls=%async_computation.2 | async-start | bytes 4194304 | tf_op jit(solution)/shard_map/all_to_all | solution.py:61
  174.8 217.2 %all-reduce.7.cloned.1.call-start = ((), (), s32[]{:S(2)}) async-start(), calls=%async_computation.5 | async-start | bytes 1048576 | tf_op jit(solution)/shard_map/psum | solution.py:44
  176.3 268.6 %all-reduce.11.cloned.1.call-start = ((), (), s32[]{:S(2)}) async-start(), calls=%async_computation.7 | async-start | bytes 262144 | tf_op jit(solution)/shard_map/psum | solution.py:73
  233.4 1.5 copy-start.1
  233.4 158.6 %copy-start.3 = (s32[2,512,256]{2,1,0:T(8,128)S(1)}, s32[2,512,256]{2,1,0:T(8,128)}, u32[]{:S(2)}) copy-start(s32[2,512,256]{2,1,0:T(8,128)} %param.10) | copy-start | bytes 3145732
  394.7 175.7 %all-reduce.15.cloned.1.call-start = ((), (), s32[]{:S(2)}) async-start(), calls=%async_computation.9 | async-start | bytes 524288 | tf_op jit(solution)/shard_map/psum | solution.py:59
  571.5 1.5 copy-start.4
  575.3 14.8 %copy-start.7 = (f32[128,256]{0,1:T(8,128)S(1)}, f32[128,256]{0,1:T(8,128)}, u32[]{:S(2)}) copy-start(f32[128,256]{0,1:T(8,128)} %all-reduce.11.cloned.1.call-done) | copy-start | bytes 393220
  575.3 234.0 %all-to-all-start.4 = ((f32[128,2,2048]{2,1,0:T(2,128)}), f32[128,2,2048]{2,1,0:T(2,128)}, u32[]{:S(2)}, u32[]{:S(2)}) async-start(f32[128,2,2048]{2,1,0:T(2,128)} %all_to_all.53), calls=%async_computation.4 | async-start | bytes 4194304 | tf_op jit(solution)/shard_map/all_to_all | solution.py:61
  590.0 1.5 slice-start
  590.0 217.3 %all-reduce.13.cloned.1.call-start = ((), (), s32[]{:S(2)}) async-start(), calls=%async_computation.8 | async-start | bytes 1048576 | tf_op jit(solution)/shard_map/psum | solution.py:44
  591.5 277.3 %all-reduce.17.cloned.1.call-start = ((), (), s32[]{:S(2)}) async-start(), calls=%async_computation.10 | async-start | bytes 262144 | tf_op jit(solution)/shard_map/psum | solution.py:73
  813.9 3.4 copy-start.2
Sparse Core Ops, SparseCore 0:
  109.4 45.6 all-reduce.8
  394.8 50.0 all-reduce.10
  525.5 44.8 all-reduce.14
  818.7 50.0 all-reduce.16
Sparse Core Ops, SparseCore 1:
  179.4 212.5 all-reduce.6
  594.6 212.6 all-reduce.12
where the time goes:
time: 879 us; the launch traced here: 878 us
  waiting for transfers between devices  669 us (76%)
  blocking collectives  68.3 us (8%)
  starting transfers between devices  57.3 us (7%)
  local copies, waits for them, and re-layouts  42.6 us (5%)
  matrix products  18 us (2%)
  between operations  15.5 us (2%)
    psum x2, waiting for transfers between devices, local(): lax.psum(hub_part, 'dom') * hub_mask[trip_index].astype(jnp.float32)  371 us
    psum x2, waiting for transfers between devices, local(): gradient = lax.psum(user_part, 'hub')  99.4 us
    psum x2, waiting for transfers between devices, local(): lax.psum(tail_part, 'hub') * tail_mask[trip_index].astype(jnp.float32)  90.8 us
    all_to_all x1, blocking collectives, local(): lax.all_to_all(outgoing, 'dom', split_axis=0, concat_axis=0, tiled=True)  68.3 us
    all_to_all x1, waiting for transfers between devices, local(): lax.all_to_all(outgoing, 'dom', split_axis=0, concat_axis=0, tiled=True)  52.4 us
    all_to_all x2, waiting for transfers between devices, local(): lax.all_to_all(answer, 'dom', split_axis=0, concat_axis=0, tiled=True)  52.4 us
    all_to_all x2, starting transfers between devices, local(): lax.all_to_all(answer, 'dom', split_axis=0, concat_axis=0, tiled=True)  29.7 us
  transfers between devices with their start and end apart: 10, of which 9 were waited for; matrix products, arithmetic and copies ran while one was open for 2% of the time, Pallas kernels for 0%

commit v1 on v0

--- a/solution.py
+++ b/solution.py
@@ -4,6 +4,10 @@
 from jax.sharding import PartitionSpec as P
 
 PRECISE = lax.Precision.HIGHEST
+
+
+def make_the_classes(sheet):
+    return lax.all_gather(sheet, "hub").sum(axis=0)
 
 
 def local(user_cot, hub_adj, tiles, tile_index, hub_mask, tail_mask):
@@ -70,7 +74,7 @@
             precision=PRECISE,
             preferred_element_type=jnp.float32,
         )
-        gradient = lax.psum(user_part, "hub")
+        gradient = make_the_classes(user_part)
     return (gradient, hub_item, tail_item)
 
 

time: 879 us -> 802 us (0.912)
  the two profiles are of different devices: /device:TPU:8 before, /device:TPU:26 now
where the time goes in v1:
time: 802 us; the launch traced here: 801 us
  waiting for transfers between devices  575 us (72%)
  blocking collectives  88.3 us (11%)
  starting transfers between devices  58.3 us (7%)
  local copies, waits for them, and re-layouts  42 us (5%)
  matrix products  15.8 us (2%)
  between operations  15.8 us (2%)
    psum x2, waiting for transfers between devices, local(): lax.psum(hub_part, 'dom') * hub_mask[trip_index].astype(jnp.float32)  378 us
    psum x2, waiting for transfers between devices, local(): lax.psum(tail_part, 'hub') * tail_mask[trip_index].astype(jnp.float32)  92.5 us
    all_to_all x1, blocking collectives, local(): lax.all_to_all(outgoing, 'dom', split_axis=0, concat_axis=0, tiled=True)  61.4 us
    all_to_all x2, waiting for transfers between devices, local(): lax.all_to_all(answer, 'dom', split_axis=0, concat_axis=0, tiled=True)  50.8 us
    all_to_all x1, waiting for transfers between devices, local(): lax.all_to_all(outgoing, 'dom', split_axis=0, concat_axis=0, tiled=True)  50.8 us
    all_to_all x2, starting transfers between devices, local(): lax.all_to_all(answer, 'dom', split_axis=0, concat_axis=0, tiled=True)  29.4 us
    all_gather x2, blocking collectives, make_the_classes(): return lax.all_gather(sheet, 'hub').sum(axis=0)  26.9 us
    all_to_all x1, starting transfers between devices, local(): lax.all_to_all(slot_block, 'dom', split_axis=0, concat_axis=0, tiled=True)  17.1 us
  transfers between devices with their start and end apart: 8, of which 7 were waited for; matrix products, arithmetic and copies ran while one was open for 2% of the time, Pallas kernels for 0%

profile of v1, /device:TPU:26, one launch (start us, length us, event | category | flops | bytes accessed | tf_op | source)
XLA Modules:
  0.0 801.2 jit_solution(16757923567548699545)
XLA Ops:
  8.0 0.8 slice_bitcast_fusion
  9.6 1.0 scatter_custom_fusion
  10.6 0.8 all_to_all.41
  11.4 17.1 %all-to-all-start = ((s32[128,2,1]{1,2,0:T(1,128)}), s32[128,2,1]{1,2,0:T(1,128)S(1)}, u32[]{:S(2)}, u32[]{:S(2)}) async-start(s32[128,2,1]{1,2,0:T(1,128)} %bitcast.9), calls=%async_computation | async-start | bytes 131072 | tf_op jit(solution)/shard_map/all_to_all | solution.py:58
  29.2 2.1 fusion.12
  31.5 1.7 scatter_custom_fusion.1
  33.2 2.3 all_to_all.43
  35.5 2.2 all-to-all-done
  37.8 11.5 %all-to-all-start.1 = ((f32[128,2,2048]{2,1,0:T(2,128)}), f32[128,2,2048]{2,1,0:T(2,128)S(1)}, u32[]{:S(2)}, u32[]{:S(2)}) async-start(f32[128,2,2048]{2,1,0:T(2,128)} %all_to_all.43), calls=%async_computation.1 | async-start | bytes 4194304 | tf_op jit(solution)/shard_map/all_to_all | solution.py:57
  49.8 0.8 reduce.5
  50.9 50.8 %all-to-all-done.1 = f32[128,2,2048]{2,1,0:T(2,128)S(1)} async-done(((f32[128,2,2048]{2,1,0:T(2,128)}), f32[128,2,2048]{2,1,0:T(2,128)S(1)}, u32[]{:S(2)}, u32[]{:S(2)}) %all-to-all-start.1) | async-done | bytes 2097184 | tf_op jit(solution)/shard_map/all_to_all | solution.py:57
  101.7 2.5 all_to_all.45
  104.2 2.5 fusion.26
  107.5 46.3 %all-reduce.7.cloned.1.call-done = f32[256,256]{1,0:T(8,128)} async-done(((f32[256,256]{1,0:T(8,128)}), f32[256,256]{1,0:T(8,128)}) %all-reduce.7.cloned.1.call-update) | async-done | bytes 262160 | tf_op jit(solution)/shard_map/psum | solution.py:63
  153.8 1.0 bitcast_multiply_fusion.4
  154.9 1.5 gather_fusion
  156.3 2.2 all_to_all.47
  158.6 14.9 %all-to-all-start.2 = ((f32[128,2,2048]{2,1,0:T(2,128)}), f32[128,2,2048]{2,1,0:T(2,128)}, u32[]{:S(2)}, u32[]{:S(2)}) async-start(f32[128,2,2048]{2,1,0:T(2,128)} %all_to_all.47), calls=%async_computation.2 | async-start | bytes 4194304 | tf_op jit(solution)/shard_map/all_to_all | solution.py:65
  173.5 1.4 fusion.33
  175.0 50.8 %all-to-all-done.2 = f32[128,2,2048]{2,1,0:T(2,128)} async-done(((f32[128,2,2048]{2,1,0:T(2,128)}), f32[128,2,2048]{2,1,0:T(2,128)}, u32[]{:S(2)}, u32[]{:S(2)}) %all-to-all-start.2) | async-done | bytes 2097184 | tf_op jit(solution)/shard_map/all_to_all | solution.py:65
  225.9 2.7 all_to_all.49
  228.6 1.9 gather_fusion.1
  230.5 1.5 reshape.128
  232.0 2.0 fusion.10
  234.0 159.9 %all-reduce.5.cloned.1.call-done = f32[512,256]{1,0:T(8,128)} async-done(((f32[512,256]{1,0:T(8,128)}), f32[512,256]{1,0:T(8,128)}) %all-reduce.5.cloned.1.call-update) | async-done | bytes 524304 | tf_op jit(solution)/shard_map/psum | solution.py:48
  393.9 2.0 fusion.1
  395.9 13.5 %all-gather = f32[512,256]{0,1:T(8,128)S(1)} all-gather(f32[128,256]{0,1:T(8,128)S(1)} %fusion.1), channel_id=2, replica_groups=mesh['dom'=128,'hub'=4] {'hub'}, dimensions={0}, use_global_device_ids=true | all-gather | bytes 655360 | tf_op jit(solution)/shard_map/all_gather | solution.py:10
  409.9 1.0 fusion.8
  410.9 1.1 reshape.186
  412.0 2.4 scatter_custom_fusion.2
  414.5 2.3 all_to_all.50
  416.8 61.4 %all_to_all.61 = f32[128,2,2048]{2,1,0:T(2,128)} all-to-all(f32[128,2,2048]{2,1,0:T(2,128)} %all_to_all.50), channel_id=1, replica_groups=mesh['dom'=128,'hub'=4] {'dom'}, dimensions={0} | all-to-all | bytes 4194304 | tf_op jit(solution)/shard_map/all_to_all | solution.py:57
  478.2 2.7 all_to_all.52
  480.9 0.9 fusion.25
  482.5 46.1 %all-reduce.11.cloned.1.call-done = f32[256,256]{1,0:T(8,128)} async-done(((f32[256,256]{1,0:T(8,128)}), f32[256,256]{1,0:T(8,128)}) %all-reduce.11.cloned.1.call-update) | async-done | bytes 262160 | tf_op jit(solution)/shard_map/psum | solution.py:63
  528.6 1.1 bitcast_multiply_fusion.3
  529.8 1.5 gather_fusion.2
  531.2 2.2 all_to_all.53
  533.5 14.6 %all-to-all-start.4 = ((f32[128,2,2048]{2,1,0:T(2,128)}), f32[128,2,2048]{2,1,0:T(2,128)}, u32[]{:S(2)}, u32[]{:S(2)}) async-start(f32[128,2,2048]{2,1,0:T(2,128)} %all_to_all.53), calls=%async_computation.4 | async-start | bytes 4194304 | tf_op jit(solution)/shard_map/all_to_all | solution.py:65
  548.1 1.4 convolution_bitcast_fusion
  549.7 218.6 %all-reduce.9.cloned.1.call-done = f32[512,256]{0,1:T(8,128)} async-done(((f32[512,256]{0,1:T(8,128)}), f32[512,256]{0,1:T(8,128)}) %all-reduce.9.cloned.1.call-update) | async-done | bytes 524304 | tf_op jit(solution)/shard_map/psum | solution.py:48
  768.3 1.1 bitcast_multiply_fusion
  769.4 1.0 copy.28
  770.4 2.7 all_to_all.55
  773.1 1.9 gather_fusion.3
  775.1 1.4 reshape.132
  776.5 2.0 fusion.6
  779.1 13.5 %all-gather.1 = f32[512,256]{0,1:T(8,128)S(1)} all-gather(f32[128,256]{0,1:T(8,128)S(1)} %fusion), channel_id=3, replica_groups=mesh['dom'=128,'hub'=4] {'hub'}, dimensions={0}, use_global_device_ids=true | all-gather | bytes 655360 | tf_op jit(solution)/shard_map/all_gather | solution.py:10
  (48 shorter events, 6.9 us)
Async XLA Ops:
  8.0 165.5 %copy-start = (f32[128,512]{1,0:T(8,128)S(1)}, f32[128,512]{1,0:T(8,128)}, u32[]{:S(2)}) copy-start(f32[128,512]{1,0:T(8,128)} %param.7) | copy-start | bytes 786436
  11.4 26.4 %all-to-all-start = ((s32[128,2,1]{1,2,0:T(1,128)}), s32[128,2,1]{1,2,0:T(1,128)S(1)}, u32[]{:S(2)}, u32[]{:S(2)}) async-start(s32[128,2,1]{1,2,0:T(1,128)} %bitcast.9), calls=%async_computation | async-start | bytes 131072 | tf_op jit(solution)/shard_map/all_to_all | solution.py:58
  37.8 63.9 %all-to-all-start.1 = ((f32[128,2,2048]{2,1,0:T(2,128)}), f32[128,2,2048]{2,1,0:T(2,128)S(1)}, u32[]{:S(2)}, u32[]{:S(2)}) async-start(f32[128,2,2048]{2,1,0:T(2,128)} %all_to_all.43), calls=%async_computation.1 | async-start | bytes 4194304 | tf_op jit(solution)/shard_map/all_to_all | solution.py:57
  49.3 104.6 %all-reduce.7.cloned.1.call-start = ((), (), s32[]{:S(2)}) async-start(), calls=%async_computation.6 | async-start | bytes 524288 | tf_op jit(solution)/shard_map/psum | solution.py:63
  104.2 49.7 %copy-start.6 = (s32[2,256,256]{2,1,0:T(8,128)S(1)}, s32[2,256,256]{2,1,0:T(8,128)}, u32[]{:S(2)}) copy-start(s32[2,256,256]{2,1,0:T(8,128)} %param.11) | copy-start | bytes 1572868
  158.6 15.0 %copy-start.7 = (f32[128,256]{1,0:T(8,128)S(1)}, f32[128,256]{1,0:T(8,128)}, u32[]{:S(2)}) copy-start(f32[128,256]{1,0:T(8,128)} %param.6) | copy-start | bytes 393220
  158.6 67.3 %all-to-all-start.2 = ((f32[128,2,2048]{2,1,0:T(2,128)}), f32[128,2,2048]{2,1,0:T(2,128)}, u32[]{:S(2)}, u32[]{:S(2)}) async-start(f32[128,2,2048]{2,1,0:T(2,128)} %all_to_all.47), calls=%async_computation.2 | async-start | bytes 4194304 | tf_op jit(solution)/shard_map/all_to_all | solution.py:65
  173.5 220.4 %all-reduce.5.cloned.1.call-start = ((), (), s32[]{:S(2)}) async-start(), calls=%async_computation.5 | async-start | bytes 1048576 | tf_op jit(solution)/shard_map/psum | solution.py:48
  175.0 353.7 %all-reduce.11.cloned.1.call-start = ((), (), s32[]{:S(2)}) async-start(), calls=%async_computation.8 | async-start | bytes 524288 | tf_op jit(solution)/shard_map/psum | solution.py:63
  230.5 1.5 copy-start.1
  230.5 163.3 %copy-start.4 = (s32[2,512,256]{2,1,0:T(8,128)S(1)}, s32[2,512,256]{2,1,0:T(8,128)}, u32[]{:S(2)}) copy-start(s32[2,512,256]{2,1,0:T(8,128)} %param.10) | copy-start | bytes 3145732
  529.7 1.5 copy-start.5
  533.5 237.0 %all-to-all-start.4 = ((f32[128,2,2048]{2,1,0:T(2,128)}), f32[128,2,2048]{2,1,0:T(2,128)}, u32[]{:S(2)}, u32[]{:S(2)}) async-start(f32[128,2,2048]{2,1,0:T(2,128)} %all_to_all.53), calls=%async_computation.4 | async-start | bytes 4194304 | tf_op jit(solution)/shard_map/all_to_all | solution.py:65
  548.1 1.5 slice-start
  548.1 220.2 %all-reduce.9.cloned.1.call-start = ((), (), s32[]{:S(2)}) async-start(), calls=%async_computation.7 | async-start | bytes 1048576 | tf_op jit(solution)/shard_map/psum | solution.py:48
  769.4 1.0 copy-start.2
  775.1 3.4 copy-start.3
Sparse Core Ops, SparseCore 0:
  107.6 46.2 all-reduce.6
  482.6 45.9 all-reduce.10
Sparse Core Ops, SparseCore 1:
  178.1 215.7 all-reduce.4
  552.4 215.9 all-reduce.8
